TPU v7x, 256 devices: a whole 4x4x8 slice. The times are simulated.
256 devices in a mesh: role: 2 (over x_hi), ctx: 16 (over z, core), tp: 8 (over x_lo, y).
Axes of the slice: x: 4 (x_hi: 2, x_lo: 2; x = x_hi * 2 + x_lo), y: 4, z: 8, core: 2. Of those that a mesh axis runs over, the one named last changes fastest.
Arguments:
- prefill_query: bfloat16 [2, 1024, 12288], P('role', 'ctx', 'tp'), may hold values from -130 to 130
- prefix_kv: bfloat16 [2, 2, 4096, 1024], P('role', None, 'ctx', 'tp'), may hold values from -6 to 6
- new_kv: bfloat16 [2, 2, 1024, 1024], P('role', None, 'ctx', 'tp'), may hold values from -6 to 6
- new_exponent: int32 [2, 2, 64, 8], P('role', None, 'ctx', 'tp'), may hold values from -3 to 2
- block_shift: int32 [2, 4], replicated, may hold values from 0 to 15, as said below
- decode_query: bfloat16 [2, 32, 12288], P('role', 'ctx', 'tp'), may hold values from -200 to 200
- decode_cache: bfloat16 [2, 2, 32, 2048, 1024], P('role', None, 'ctx', None, 'tp'), may hold values from -6 to 6
- cache_exponent: int32 [2, 2, 32, 16, 8], P('role', None, 'ctx', None, 'tp'), may hold values from -1 to 2
- cache_length: int32 [2, 32], P('role', 'ctx'), may hold values from 1 to 2048, 32768 in all within a row
- decode_new_kv: bfloat16 [2, 2, 32, 1024], P('role', None, 'ctx', 'tp'), may hold values from -6 to 6
- out_weight: bfloat16 [12288, 12288], P('tp', 'ctx'), may hold values from -0.5 to 0.5
- decode_residual: bfloat16 [2, 32, 12288], P('role', 'tp', 'ctx'), may hold values from -6 to 6
Outputs:
- prefill_attn: bfloat16 [2, 1024, 12288], P('role', 'ctx', 'tp')
- shipped: bfloat16 [2, 2, 1024, 1024], P('role', None, 'ctx', 'tp')
- decode_out: bfloat16 [2, 32, 12288], P('role', 'tp', 'ctx')
Inputs may be any that keep to these rules, and one draw needn't show every extreme that they name: The 4 values of block_shift of one group are distinct; block j of every prefill shard c of group g goes to decode owner (c + block_shift[g, j]) mod 16 of the other group.
All inputs are finite; a program needn't handle non-finite values. No bound on the sum of `cache_length` on one device may be relied on, other than what follows from the above.
Results may differ from a plain program's by a relative error of at most 0.018.
Values may be sent and summed in bfloat16 or wider, within the bound.
A program may use at most 64 MiB of HBM per device.

v0:
```python
import jax
import jax.numpy as jnp
from jax import lax
from jax.sharding import PartitionSpec as P

HEADS = 96
KEY_VALUE_HEADS = 8
HEAD_DIM = 128
CBLK = 128


NEG = -1e30


def swapped(array, axis, distance):
    return lax.ppermute(array, axis, [(i, i ^ 1 << distance) for i in range(lax.axis_size(axis))])


def blend(carry, scores, visible, values):
    acc, top, total = carry
    masked = jnp.where(visible, scores, NEG)
    fresh = jnp.maximum(top, jnp.max(masked, axis=-1))
    attention_weights = jnp.where(visible, jnp.exp(masked - fresh[..., None]), 0.0)
    keep = jnp.exp(top - fresh)
    total = total * keep + jnp.sum(attention_weights, axis=-1)
    acc = acc * keep[..., None] + jnp.einsum(
        "krs,skd->krd",
        attention_weights.astype(jnp.bfloat16),
        values,
        preferred_element_type=jnp.float32,
    )
    return (acc, fresh, total)


def per_device(
    prefill_query,
    prefix_kv,
    new_kv,
    new_exponent,
    block_shift,
    decode_query,
    decode_cache,
    cache_exponent,
    cache_length,
    decode_new_kv,
    out_weight,
    decode_residual,
):
    head_dim = HEAD_DIM
    group_size = HEADS // KEY_VALUE_HEADS
    score_scale = head_dim ** (-0.5)
    stretch = prefill_query.shape[1]
    kv_local = prefix_kv.shape[3] // head_dim
    pre_rows = prefix_kv.shape[2]
    span = pre_rows + stretch
    place = lax.axis_index("ctx")
    count = lax.axis_size("ctx")
    rows_q = stretch * group_size
    queries = (
        prefill_query[0]
        .reshape(stretch, kv_local, group_size, head_dim)
        .transpose(1, 0, 2, 3)
        .reshape(kv_local, rows_q, head_dim)
    )
    query_pos = place * stretch + jnp.arange(rows_q, dtype=jnp.int32) // group_size
    local_kv = jnp.concatenate([prefix_kv, new_kv], axis=2)
    lead = ()
    carry = (
        jnp.zeros(lead + (kv_local, rows_q, head_dim), jnp.float32),
        jnp.full(lead + (kv_local, rows_q), NEG, jnp.float32),
        jnp.zeros(lead + (kv_local, rows_q), jnp.float32),
    )
    piece = lax.all_gather(local_kv, "ctx", axis=2, tiled=True)
    start = jnp.int32(0)
    width = piece.shape[2]
    step = min(width, 1024)
    for first in range(0, width, step):
        size = min(step, width - first)
        keys = piece[0, 0, first : first + size].reshape(size, kv_local, head_dim)
        values = piece[0, 1, first : first + size].reshape(size, kv_local, head_dim)
        index = start + first + jnp.arange(size, dtype=jnp.int32)
        device = index // span
        within = index % span
        newpos = device * stretch + within - pre_rows
        visible = (within < pre_rows)[None, :] | (newpos[None, :] <= query_pos[:, None])
        scores = (
            jnp.einsum("krd,skd->krs", queries, keys, preferred_element_type=jnp.float32)
            * score_scale
        )
        carry = blend(carry, scores, visible[None], values)
    acc, top, total = carry
    layer_output = acc / total[..., None]
    prefill_attn = (
        layer_output.reshape(kv_local, stretch, group_size, head_dim)
        .transpose(1, 0, 2, 3)
        .reshape(1, stretch, kv_local * group_size * head_dim)
        .astype(jnp.bfloat16)
    )
    role = lax.axis_index("role")
    blocks_dev = new_exponent.shape[2]
    block_len = stretch // blocks_dev
    factor_new = jnp.exp2(-new_exponent[0].astype(jnp.float32))
    raw = new_kv[0].reshape(2, blocks_dev, block_len, kv_local, head_dim).astype(jnp.float32)
    codes = (
        (raw * factor_new[:, :, None, :, None])
        .astype(jnp.bfloat16)
        .reshape(2, blocks_dev, block_len, kv_local * head_dim)
    )
    mine = jnp.take(block_shift, role, axis=0)
    theirs = jnp.take(block_shift, 1 - role, axis=0)
    targets = jnp.arange(count, dtype=jnp.int32)
    route = ((place + mine)[None, :] % count == targets[:, None]).astype(jnp.bfloat16)
    outgoing = jnp.einsum("nj,kjbe->nkbe", route, codes, preferred_element_type=jnp.float32).astype(
        jnp.bfloat16
    )
    crossed = swapped(outgoing, "role", 0)
    arrived = lax.all_to_all(crossed, "ctx", split_axis=0, concat_axis=0, tiled=True)
    pick = ((place - theirs)[:, None] % count == targets[None, :]).astype(jnp.bfloat16)
    slots = jnp.einsum("jn,nkbe->kjbe", pick, arrived, preferred_element_type=jnp.float32).astype(
        jnp.bfloat16
    )
    shipped = slots.reshape(1, 2, blocks_dev * block_len, kv_local * head_dim)
    requests = decode_query.shape[1]
    cache_len = decode_cache.shape[3]
    decoding_query = decode_query[0].reshape(requests, kv_local, group_size, head_dim)
    powers = jnp.exp2(cache_exponent[0].astype(jnp.float32)).astype(jnp.bfloat16)
    plain = (
        decode_cache[0].reshape(2, requests, cache_len // CBLK, CBLK, kv_local, head_dim)
        * powers[:, :, :, None, :, None]
    ).reshape(2, requests, cache_len, kv_local, head_dim)
    self_score = decode_new_kv[0].reshape(2, requests, kv_local, head_dim)
    scores = (
        jnp.einsum("bkgd,bskd->bkgs", decoding_query, plain[0], preferred_element_type=jnp.float32)
        * score_scale
    )
    own_score = (
        jnp.einsum(
            "swcl,swl->swc", decoding_query, self_score[0], preferred_element_type=jnp.float32
        )
        * score_scale
    )
    live = (jnp.arange(cache_len, dtype=jnp.int32)[None, :] < cache_length[0][:, None])[
        :, None, None, :
    ]
    masked = jnp.where(live, scores, NEG)
    top = jnp.maximum(jnp.max(masked, axis=-1), own_score)
    attention_weights = jnp.where(live, jnp.exp(masked - top[..., None]), 0.0)
    self_weight = jnp.exp(own_score - top)
    total = jnp.sum(attention_weights, axis=-1) + self_weight
    acc = jnp.einsum(
        "bkgs,bskd->bkgd",
        attention_weights.astype(jnp.bfloat16),
        plain[1],
        preferred_element_type=jnp.float32,
    )
    acc = acc + jnp.einsum(
        "pah,paw->pahw",
        self_weight.astype(jnp.bfloat16),
        self_score[1],
        preferred_element_type=jnp.float32,
    )
    decode_attn = (
        (acc / total[..., None])
        .astype(jnp.bfloat16)
        .reshape(requests, kv_local * group_size * head_dim)
    )
    terms = jnp.dot(
        lax.all_gather(decode_attn, "ctx", axis=0, tiled=True),
        out_weight,
        preferred_element_type=jnp.float32,
    )
    summed = lax.psum_scatter(
        terms.astype(jnp.bfloat16), "tp", scatter_dimension=0, tiled=True
    ).astype(jnp.float32)
    decode_out = (decode_residual[0].astype(jnp.float32) + summed).astype(jnp.bfloat16)[None]
    return (prefill_attn, shipped, decode_out)


def solution(mesh):
    placed = (
        P("role", "ctx", "tp"),
        P("role", None, "ctx", "tp"),
        P("role", None, "ctx", "tp"),
        P("role", None, "ctx", "tp"),
        P(),
        P("role", "ctx", "tp"),
        P("role", None, "ctx", None, "tp"),
        P("role", None, "ctx", None, "tp"),
        P("role", "ctx"),
        P("role", None, "ctx", "tp"),
        P("tp", "ctx"),
        P("role", "tp", "ctx"),
    )
    return jax.shard_map(
        per_device,
        mesh=mesh,
        in_specs=placed,
        out_specs=(P("role", "ctx", "tp"), P("role", None, "ctx", "tp"), P("role", "tp", "ctx")),
        check_vma=False,
    )
```

profile of v0, /device:TPU:2, one launch (start us, length us, event | category | flops | bytes accessed | tf_op | source)
XLA Modules:
  0.0 112.5 jit_solution(12359120307851591524)
XLA Ops:
  7.2 0.0 copy-start
  7.2 0.0 all-gather.3.cloned.1.call-start
  7.2 1.8 %pad_maximum_fusion = bf16[1,2,320,128]{3,2,1,0:T(8,128)(2,1)} fusion(bf16[1,2,64,128]{3,2,1,0:T(8,128)(2,1)} %param.16, bf16[1,2,256,128]{3,2,1,0:T(8,128)(2,1)} %param.15), kind=kLoop, calls=%fused_computation.70 | loop fusion | flops 327680 | bytes 327680 | tf_op jit(solution)/shard_map/concatenate | solution.py:66
  9.0 0.0 all-gather.3.cloned.1.call-update
  9.0 0.8 convert.13
  9.8 0.8 and_select_fusion
  10.5 0.7 multiply_exponential_fusion
  11.2 0.3 convolution_convert_fusion
  11.6 2.2 %collective-permute-start = (bf16[16,2,16,128]{3,0,2,1:T(8,128)(2,1)S(1)}, bf16[16,2,16,128]{3,0,2,1:T(8,128)(2,1)S(1)}, u32[]{:S(2)}, u32[]{:S(2)}) collective-permute-start(bf16[16,2,16,128]{3,0,2,1:T(8,128)(2,1)S(1)} %convolution_convert_fusion), channel_id=1, source_target_pairs={{0,128},{128,0},{1,129},{129,1},{2,130},{130,2},{3,131},{131,3},{4... | collective-permute-start | bytes 393224 | tf_op jit(solution)/shard_map/ppermute | solution.py:16
  13.8 0.7 exponential_convert_fusion
  14.5 0.7 reshape.665
  15.2 0.7 bitcast_convert_fusion
  15.9 0.1 fusion.123
  16.0 1.8 %broadcast_multiply_fusion = bf16[2,2,16,128,1,128]{5,3,2,1,4,0:T(8,128)(2,1)S(1)} fusion(bf16[2,2,16,128,1,128]{5,3,2,1,4,0:T(8,128)(2,1)} %bitcast.160, bf16[2,2,16]{2,1,0:T(2,128)(2,1)S(1)} %bitcast.163), kind=kLoop, calls=%fused_computation.51 | loop fusion | flops 1048576 | bytes 4194432 | tf_op jit(solution)/shard_map/mul | solution.py:128
  17.8 0.0 copy-start.4
  17.8 0.2 fusion.143
  18.0 0.4 copy-done.4
  18.4 0.1 iota_compare_fusion
  18.5 0.0 copy-start.2
  18.5 0.0 copy-start.5
  18.5 0.0 copy-start.3
  18.6 0.5 fusion.144
  19.0 0.2 fusion.58
  19.3 0.3 fusion.52
  19.6 20.3 %all-gather = bf16[16,2,1536]{2,1,0:T(2,128)(2,1)S(1)} all-gather(bf16[1,2,1536]{2,1,0:T(2,128)(2,1)S(1)} %reshape.716), channel_id=1, replica_groups=mesh['role'=2,'ctx'=16,'tp'=8] {'ctx'}, dimensions={0}, use_global_device_ids=true | all-gather | bytes 104448 | tf_op jit(solution)/shard_map/all_gather | solution.py:168
  40.0 0.0 copy-done
  40.0 0.5 convolution_convert_fusion.1
  40.6 0.0 collective-permute-done
  40.6 0.7 copy.19
  41.3 3.7 %all-to-all-start = ((bf16[16,2,16,128]{3,2,1,0:T(8,128)(2,1)}), bf16[16,2,16,128]{3,2,1,0:T(8,128)(2,1)S(1)}, u32[]{:S(2)}, u32[]{:S(2)}) async-start(bf16[16,2,16,128]{3,2,1,0:T(8,128)(2,1)} %copy.19), calls=%async_computation | async-start | bytes 262144 | tf_op jit(solution)/shard_map/all_to_all | solution.py:117
  45.0 34.9 %all-reduce = bf16[32,768]{1,0:T(8,128)(2,1)S(1)} all-reduce(bf16[32,768]{1,0:T(8,128)(2,1)S(1)} %convolution_convert_fusion.1), channel_id=2, replica_groups=mesh['role'=2,'ctx'=16,'tp'=8] {'tp'}, use_global_device_ids=true, to_apply=%region_12.14.clone | all-reduce | flops 24576 | bytes 98304
  79.9 0.0 copy-done.2
  79.9 0.3 reshape.653
  80.2 0.0 copy-done.5
  80.2 0.6 dynamic-slice.7
  81.4 0.0 copy-done.3
  81.4 0.6 fusion.69
  82.0 0.0 all-to-all-done
  82.0 0.2 fusion.50
  82.2 0.6 copy.21
  82.9 0.0 all-gather.3.cloned.1.call-done
  82.9 0.0 copy-start.1
  82.9 1.7 %fusion.55 = f32[1024,768]{1,0:T(8,128)S(1)} fusion(bf16[768,128]{1,0:T(8,128)(2,1)S(1)} %reshape.653, bf16[1,2,5120,128]{3,2,1,0:T(8,128)(2,1)} %all-gather.3.cloned.1.call-done), kind=kOutput, calls=%fused_computation.60 | convolution fusion | flops 201326592 | bytes 3604480 | tf_op jit(solution)/shard_map/krd,skd->krs/dot_general | solution.py:87
  84.5 0.1 copy-done.1
  84.7 0.6 fusion.56
  85.3 0.6 fusion.57
  85.8 3.2 %fusion.3 = (f32[768]{0:T(1024)S(1)}, f32[768]{0:T(1024)S(1)}, f32[768]{0:T(1024)S(1)}, f32[768]{0:T(1024)S(1)}, f32[1024,768]{1,0:T(8,128)S(1)}) fusion(s32[768]{0:T(1024)S(1)} %fusion.72, s32[1024]{0:T(1024)S(1)} %get-tuple-element.50, pred[1024]{0:T(1024)(128)(4,1)S(1)} %get-tuple-element.51, f32[1024,768]{1,0:T(8,128)S(1)} %fusion.56, ...), kind=kOutput, calls=%fused_computation.18 | convolution fusion | flops 217052160 | bytes 13078528 | tf_op jit(solution)/shard_map/krd,skd->krs/dot_general | solution.py:87
  89.1 2.0 %fusion.137 = (f32[768]{0:T(1024)S(1)}, f32[768]{0:T(1024)S(1)}, f32[1024,768]{1,0:T(8,128)S(1)}) fusion(f32[768]{0:T(1024)S(1)} %get-tuple-element.30, f32[1024,768]{1,0:T(8,128)S(1)} %get-tuple-element.43, s32[768]{0:T(1024)S(1)} %fusion.72, s32[1024]{0:T(1024)S(1)} %get-tuple-element.50, pred[1024]{0:T(1024)(128)(4,1)S(1)} %get-tuple-element.51, ...), kind=kOutput, calls=%fused_computation.197 | convolution fusion | flops 210762240 | bytes 6774784 | tf_op jit(solution)/shard_map/krd,skd->krs/dot_general | solution.py:87
  91.2 6.0 %fusion.136 = (f32[768]{0:T(1024)S(1)}, f32[768]{0:T(1024)S(1)}, f32[768]{0:T(1024)S(1)}, f32[768]{0:T(1024)S(1)}) fusion(f32[768]{0:T(1024)S(1)} %get-tuple-element.36, f32[1024,768]{1,0:T(8,128)S(1)} %fusion.57, s32[768]{0:T(1024)S(1)} %fusion.72, s32[1024]{0:T(1024)S(1)} %get-tuple-element.47, pred[1024]{0:T(1024)(128)(4,1)S(1)} %get-tuple-element.54, ...), kind=kLoop, calls=%fused_computation.196 | loop fusion | flops 22017024 | bytes 12631040 | tf_op jit(solution)/shard_map/reduce_sum | solution.py:25
  97.2 1.4 %fusion.13 = f32[768,128]{1,0:T(8,128)S(1)} fusion(bf16[1,2,5120,128]{3,2,1,0:T(8,128)(2,1)S(1)} %copy-done.1, f32[1024,768]{1,0:T(8,128)S(1)} %fusion.56, f32[768]{0:T(1024)S(1)} %get-tuple-element.32, s32[768]{0:T(1024)S(1)} %fusion.72, s32[1024]{0:T(1024)S(1)} %get-tuple-element.48, pred[1024]{0:T(1024)(128)(4,1)S(1)} %get-tuple-element.53), kind=kOutput, calls=%fused_computation.29 | convolution fusion | flops 206831616 | bytes 3814400 | tf_op jit(solution)/shard_map/krs,skd->krd/dot_general | solution.py:26
  98.7 1.4 %fusion.11 = f32[768,128]{1,0:T(8,128)S(1)} fusion(bf16[1,2,5120,128]{3,2,1,0:T(8,128)(2,1)S(1)} %copy-done.1, f32[1024,768]{1,0:T(8,128)S(1)} %fusion.55, f32[768]{0:T(1024)S(1)} %get-tuple-element.31, s32[768]{0:T(1024)S(1)} %fusion.72, s32[1024]{0:T(1024)S(1)} %get-tuple-element.49, pred[1024]{0:T(1024)(128)(4,1)S(1)} %get-tuple-element.52), kind=kOutput, calls=%fused_computation.27 | convolution fusion | flops 206831616 | bytes 3814400 | tf_op jit(solution)/shard_map/krs,skd->krd/dot_general | solution.py:26
  100.1 1.4 %fusion.7 = f32[768,128]{1,0:T(8,128)S(1)} fusion(bf16[1,2,5120,128]{3,2,1,0:T(8,128)(2,1)S(1)} %copy-done.1, f32[1024,768]{1,0:T(8,128)S(1)} %get-tuple-element.44, f32[768]{0:T(1024)S(1)} %max.123, s32[768]{0:T(1024)S(1)} %fusion.72, s32[1024]{0:T(1024)S(1)} %fusion.86, pred[1024]{0:T(1024)(128)(4,1)S(1)} %fusion.92), kind=kOutput, calls=%fused_computation.23 | convolution fusion | flops 206831616 | bytes 3814400 | tf_op jit(solution)/shard_map/krs,skd->krd/dot_general | solution.py:26
  101.5 1.7 %fusion.44 = f32[768,128]{1,0:T(8,128)S(1)} fusion(f32[768,128]{1,0:T(8,128)S(1)} %fusion.11, f32[768,128]{1,0:T(8,128)S(1)} %fusion.13, bf16[1,2,5120,128]{3,2,1,0:T(8,128)(2,1)S(1)} %copy-done.1, f32[768]{0:T(1024)S(1)} %get-tuple-element.29, f32[768]{0:T(1024)S(1)} %get-tuple-element.28, f32[768]{0:T(1024)S(1)} %get-tuple-element.27, ...), kind=kOutput, calls=%fused_computation.42 | convolution fusion | flops 207421440 | bytes 4617216 | tf_op jit(solution)/shard_map/krs,skd->krd/dot_general | solution.py:26
  103.2 1.5 %fusion.47 = bf16[768,128]{1,0:T(8,128)(2,1)S(1)} fusion(f32[768,128]{1,0:T(8,128)S(1)} %fusion.7, f32[768,128]{1,0:T(8,128)S(1)} %fusion.44, bf16[1,2,5120,128]{3,2,1,0:T(8,128)(2,1)S(1)} %copy-done.1, f32[768]{0:T(1024)S(1)} %get-tuple-element.25, f32[768]{0:T(1024)S(1)} %get-tuple-element.26, f32[1024,768]{1,0:T(8,128)S(1)} %get-tuple-element.43, ...), kind=kOutput, calls=%fused_computation.43 | convolution fusion | flops 207323136 | bytes 4412416 | tf_op jit(solution)/shard_map/krs,skd->krd/dot_general | solution.py:26
  104.7 0.9 convert_element_type.125
  (15 shorter events, 0.2 us)
Async XLA Ops:
  7.2 32.9 %copy-start = (bf16[1536,768]{1,0:T(8,128)(2,1)S(1)}, bf16[1536,768]{1,0:T(8,128)(2,1)}, u32[]{:S(2)}) copy-start(bf16[1536,768]{1,0:T(8,128)(2,1)} %param.24) | copy-start | bytes 7077892
  7.2 75.7 %all-gather.3.cloned.1.call-start = ((), (), s32[]{:S(2)}) async-start(), calls=%async_computation.1 | async-start | bytes 2785280 | tf_op jit(solution)/shard_map/all_gather | solution.py:73
  11.6 29.0 %collective-permute-start = (bf16[16,2,16,128]{3,0,2,1:T(8,128)(2,1)S(1)}, bf16[16,2,16,128]{3,0,2,1:T(8,128)(2,1)S(1)}, u32[]{:S(2)}, u32[]{:S(2)}) collective-permute-start(bf16[16,2,16,128]{3,0,2,1:T(8,128)(2,1)S(1)} %convolution_convert_fusion), channel_id=1, source_target_pairs={{0,128},{128,0},{1,129},{129,1},{2,130},{130,2},{3,131},{131,3},{4... | collective-permute-start | bytes 393224 | tf_op jit(solution)/shard_map/ppermute | solution.py:16
  17.8 0.7 copy-start.4
  18.5 61.4 %copy-start.2 = (bf16[1,64,1536]{2,1,0:T(8,128)(2,1)S(1)}, bf16[1,64,1536]{2,1,0:T(8,128)(2,1)}, u32[]{:S(2)}) copy-start(bf16[1,64,1536]{2,1,0:T(8,128)(2,1)} %param.14) | copy-start | bytes 589828
  18.5 61.6 %copy-start.5 = (u32[256]{0:T(256)S(1)}, u32[256]{0:T(256)}, u32[]{:S(2)}) copy-start(u32[256]{0:T(256)} %constant.170) | copy-start | bytes 3076
  18.5 62.9 %copy-start.3 = (bf16[1,4,768]{2,1,0:T(4,128)(2,1)S(1)}, bf16[1,4,768]{2,1,0:T(4,128)(2,1)}, u32[]{:S(2)}) copy-start(bf16[1,4,768]{2,1,0:T(4,128)(2,1)} %param.25) | copy-start | bytes 18436
  41.3 40.7 %all-to-all-start = ((bf16[16,2,16,128]{3,2,1,0:T(8,128)(2,1)}), bf16[16,2,16,128]{3,2,1,0:T(8,128)(2,1)S(1)}, u32[]{:S(2)}, u32[]{:S(2)}) async-start(bf16[16,2,16,128]{3,2,1,0:T(8,128)(2,1)} %copy.19), calls=%async_computation | async-start | bytes 262144 | tf_op jit(solution)/shard_map/all_to_all | solution.py:117
  82.9 1.8 %copy-start.1 = (bf16[1,2,5120,128]{3,2,1,0:T(8,128)(2,1)S(1)}, bf16[1,2,5120,128]{3,2,1,0:T(8,128)(2,1)}, u32[]{:S(2)}) copy-start(bf16[1,2,5120,128]{3,2,1,0:T(8,128)(2,1)} %all-gather.3.cloned.1.call-done) | copy-start | bytes 7864324
Sparse Core Ops, SparseCore 0:
  10.4 43.7 all-gather.2
where the time goes:
time: 113 us
  blocking collectives  55.2 us (49%)
  matrix products  17.6 us (16%)
  between operations  15 us (13%)
  other arithmetic  14.2 us (13%)
  starting transfers between devices  5.93 us (5%)
  local copies, waits for them, and re-layouts  4.65 us (4%)
    unnamed x1, blocking collectives  34.9 us
    all_gather x1, blocking collectives, per_device(): lax.all_gather(decode_attn, 'ctx', axis=0, tiled=True)  20.3 us
    dot_general x5, matrix products, per_device(): jnp.einsum('krd,skd->krs', queries, keys, preferred_element_type=jnp.floa...  8.11 us
    dot_general x5, matrix products, blend(): jnp.einsum('krs,skd->krd', attention_weights.astype(jnp.bfloat16), values...  7.48 us
    reduce_sum x1, other arithmetic, blend(): total = total * keep + jnp.sum(attention_weights, axis=-1)  6.01 us
    all_to_all x1, starting transfers between devices, per_device(): lax.all_to_all(crossed, 'ctx', split_axis=0, concat_axis=0, tiled=True)  3.68 us
  transfers between devices with their start and end apart: 3, of which 0 were waited for; matrix products, arithmetic and copies ran while one was open for 10% of the time, Pallas kernels for 0%

commit v1 on v0

v1 whole, which is shorter than its diff:
```python
import jax
import jax.numpy as jnp
from jax import lax
from jax.experimental import pallas as pl
from jax.experimental.pallas import tpu as pltpu
from jax.sharding import PartitionSpec as P

MESH = pl.DeviceIdType.MESH
BF16 = jnp.bfloat16
F32 = jnp.float32
HD = 128
GROUP = 12
TOK = 64
PRE = 256
HALF = PRE // 2
ROWS = GROUP * TOK
N_CTX = 16
N_TP = 8
FAC = 16
NEWR = 2 * TOK + FAC
CACHE = 2048
CBLK = 128
DOUT = 768
LOG2E = 1.4426950408889634
SCALE2 = HD**-0.5 * LOG2E
CHUNK = 256
NEG = -1e30
NT = (((1,), (1,)), ((), ()))


def column(row):
    n = row.shape[1]
    wide = jnp.broadcast_to(row.astype(F32), (n, n))
    on = lax.broadcasted_iota(jnp.int32, (n, n), 0) == lax.broadcasted_iota(jnp.int32, (n, n), 1)
    return jnp.sum(jnp.where(on, wide, 0.0), axis=1, keepdims=True)


def kernel(
    q_hbm, prefix, new, nexp, shift_in, dq, cache, cexp, clen_in, dnew, w, resid,
    out_attn, out_ship, out_dec,
    gp, gn, nraw, ne, q_in, q_rows, m_ref, acc_ref,
    dq_in, dq_rows, cache_v, ce, dn, ga, gaf, w_v, t_out, t_in, res_v, ship_out, ship_in,
    part_o, part_s, back_o, back_s, far_v, shift, clen,
    lsem, ring_s, ring_r, q_s, q_r, at_s, at_r, tp_s, tp_r, sh_s, sh_r, po_s, po_r, ps_s, ps_r, far_s, far_r,
):
    role, p, tp = lax.axis_index("role"), lax.axis_index("ctx"), lax.axis_index("tp")
    core = lax.rem(p, 2)
    z = p // 2
    right, left = lax.rem(p + 2, N_CTX), lax.rem(p + N_CTX - 2, N_CTX)
    sib = p + 1 - 2 * core

    bar = pltpu.get_barrier_semaphore()
    for d in range(1, 8):
        pl.semaphore_signal(bar, inc=1, device_id={"ctx": lax.rem(p + 2 * d, N_CTX)}, device_id_type=MESH)
    pl.semaphore_signal(bar, inc=1, device_id={"ctx": sib}, device_id_type=MESH)
    for d in range(1, N_TP):
        pl.semaphore_signal(bar, inc=1, device_id={"tp": lax.rem(tp + d, N_TP)}, device_id_type=MESH)
    for c in (p, sib):
        pl.semaphore_signal(bar, inc=1, device_id={"role": 1 - role, "ctx": c}, device_id_type=MESH)

    loads = [
        (new.at[0], nraw), (nexp.at[0], ne), (prefix.at[0], gp.at[z]),
        (dq.at[0], dq_in), (cexp.at[0], ce), (dnew.at[0], dn),
        (cache.at[0, 0], cache_v.at[0]), (cache.at[0, 1], cache_v.at[1]),
        (q_hbm.at[0], q_in), (w, w_v), (resid.at[0], res_v), (shift_in, shift), (clen_in, clen),
    ]
    ld = [pltpu.make_async_copy(s, d, lsem.at[i]) for i, (s, d) in enumerate(loads)]
    for c in ld:
        c.start()

    pl.semaphore_wait(bar, 17)

    dev = (right, left)
    kinds = {h: ((0, 1, 2), (0, 2, 1)) for h in (1, 2, 3)}
    kinds[4] = ((3, 1), (4, 2))
    slot = {}
    for dr in (0, 1):
        for h in (1, 2, 3, 4):
            for kd in kinds[h][dr]:
                slot[(dr, h, kd)] = len(slot)

    def part(src, kd):
        if kd == 0:
            return gn.at[src]
        if kd == 1:
            return gp.at[src, :, 0:HALF]
        if kd == 2:
            return gp.at[src, :, HALF:PRE]
        if kd == 3:
            return gn.at[src, 0 : TOK + FAC]
        return gn.at[src, TOK + FAC : NEWR]

    def origin(dr, h):
        return lax.rem(z + (8 - h if dr == 0 else h), 8)

    def ring_copy(src, kd, dr, h, held=None):
        i = slot[(dr, h, kd)]
        return pltpu.make_async_remote_copy(
            src_ref=part(src, kd) if held is None else held, dst_ref=part(src, kd), send_sem=ring_s.at[i], recv_sem=ring_r.at[i],
            device_id={"ctx": dev[dr]}, device_id_type=MESH,
        )

    sends = []

    def start(c):
        c.start()
        sends.append(c)

    def post(j):
        for dr in (0, 1):
            kd = kinds[1][dr][j]
            src = gn.at[z] if j == 0 else prefix.at[0, :, 0:HALF] if kd == 1 else prefix.at[0, :, HALF:PRE]
            start(ring_copy(z, kd, dr, 1, src))

    def pump(h, j):
        for dr in (0, 1):
            kd = kinds[h][dr][j]
            src = origin(dr, h)
            ring_copy(src, kd, dr, h).wait_recv()
            if h < 3:
                start(ring_copy(src, kd, dr, h + 1))
            elif h == 3:
                if kd == 0:
                    start(ring_copy(src, 3 + dr, dr, 4))
                elif kd == 1 + dr:
                    start(ring_copy(src, kd, dr, 4))

    def to_sib(src, dst, s, r):
        return pltpu.make_async_remote_copy(
            src_ref=src, dst_ref=dst, send_sem=s, recv_sem=r, device_id={"ctx": sib}, device_id_type=MESH
        )

    def decode(r):
        qr = dq_rows[16 * r : 16 * r + 16].astype(BF16)
        s = lax.dot_general(qr, cache_v[0, r], NT, preferred_element_type=F32)
        ek = jnp.exp2(column(ce[0, r])) * SCALE2
        ev = jnp.exp2(column(ce[1, r]))
        length = clen[0, r]
        lane = lax.broadcasted_iota(jnp.int32, (16, CBLK), 1)
        cols = []
        for b in range(CACHE // CBLK):
            x = s[:, b * CBLK : (b + 1) * CBLK] * ek[b : b + 1, :]
            cols.append(jnp.where(lane < length - b * CBLK, x, NEG))
        kn = dn[0, r : r + 1].astype(F32)
        vn = dn[1, r : r + 1].astype(F32)
        own = jnp.sum(qr.astype(F32) * kn, axis=1, keepdims=True) * SCALE2
        top = cols[0]
        for x in cols[1:]:
            top = jnp.maximum(top, x)
        top = jnp.maximum(jnp.max(top, axis=1, keepdims=True), own)
        tot = jnp.zeros((16, CBLK), F32)
        pv = []
        for b, x in enumerate(cols):
            e = jnp.exp2(x - top)
            tot = tot + e
            pv.append((e * ev[b : b + 1, :]).astype(BF16))
        own = jnp.exp2(own - top)
        total = jnp.sum(tot, axis=1, keepdims=True) + own
        o = jnp.dot(jnp.concatenate(pv, axis=1), cache_v[1, r], preferred_element_type=F32)
        o = o + own.astype(BF16).astype(F32) * vn
        ga[core, z, 16 * r : 16 * r + 16] = (o / total).astype(BF16)

    def attend(blocks, half, first=False, masked=False, each=None):
        for c in range(ROWS // CHUNK):
            rows = pl.ds(half * ROWS + c * CHUNK, CHUNK)
            qc = q_rows[rows]
            keys = jnp.concatenate([b[0][...] for b in blocks], axis=0)
            vals = jnp.concatenate([b[1][...] for b in blocks], axis=0)
            n = keys.shape[0]
            s = lax.dot_general(qc, keys, NT, preferred_element_type=F32)
            if masked:
                col = lax.broadcasted_iota(jnp.int32, (CHUNK, n), 1)
                key = (col // TOK) * (2 * TOK) + lax.rem(col, TOK) + core * TOK
                tok = lax.rem(lax.broadcasted_iota(jnp.int32, (CHUNK, n), 0), TOK) + (sib if half else p) * TOK
                s = jnp.where(key <= tok, s, NEG)
            top = jnp.max(s, axis=1, keepdims=True) * SCALE2
            if not first:
                before = m_ref[rows]
                top = jnp.maximum(before[:, 0:1], top)
            e = jnp.exp2(s * SCALE2 - top).astype(BF16)
            vals = jnp.concatenate([vals, jnp.ones((n, HD), BF16)], axis=1)
            o = jnp.dot(e, vals, preferred_element_type=F32)
            if not first:
                keep = jnp.exp2(before - top)
                o = o + acc_ref[rows] * jnp.concatenate([keep, keep], axis=1)
            top = jnp.broadcast_to(top, (CHUNK, HD))
            if each is not None:
                each(c, o, top)
            else:
                acc_ref[rows] = o
                m_ref[rows] = top

    def pref(src):
        return (gp.at[src, 0], gp.at[src, 1])

    post(1)
    post(2)
    ld[0].wait()
    ld[1].wait()
    gn[z, 0:TOK] = nraw[0]
    gn[z, TOK + FAC : NEWR] = nraw[1]
    fk = jnp.exp2(-column(ne[0]))
    fv = jnp.exp2(-column(ne[1]))
    fac = jnp.concatenate([fk, fv, jnp.zeros((8, 1), F32)], axis=0)
    gn[z, TOK : TOK + FAC] = jnp.broadcast_to(fac, (FAC, HD)).astype(BF16)
    post(0)
    part_s[...] = jnp.zeros(part_s.shape, F32)
    ld[8].wait()
    for h in range(GROUP):
        q_rows[h * TOK : (h + 1) * TOK, :] = q_in[:, h * HD : (h + 1) * HD]
    q_copy = to_sib(q_rows.at[0:ROWS], q_rows.at[ROWS : 2 * ROWS], q_s.at[0], q_r.at[0])
    start(q_copy)
    ld[3].wait()
    x = dq_in[...].astype(F32)
    dq_rows[...] = jnp.zeros((32, HD), F32)
    for r in range(2):
        for h in range(GROUP):
            dq_rows[16 * r + h : 16 * r + h + 1, :] = x[r : r + 1, h * HD : (h + 1) * HD]
    for i in (4, 5, 6, 7, 12):
        ld[i].wait()
    decode(0)
    decode(1)
    for d in range(1, 8):
        c = pltpu.make_async_remote_copy(
            src_ref=ga.at[core, z], dst_ref=ga.at[core, z], send_sem=at_s.at[d], recv_sem=at_r.at[d],
            device_id={"ctx": lax.rem(p + 2 * d, N_CTX)}, device_id_type=MESH,
        )
        start(c)
    pump(1, 0)
    ld[2].wait()
    attend([pref(z)], 0, first=True)
    pump(1, 1)
    pump(1, 2)
    q_copy.wait_recv()
    attend([pref(z)], 1, first=True)
    pump(2, 0)
    one = [pref(origin(0, 1)), pref(origin(1, 1))]
    attend(one, 0)

    for d in range(1, 8):
        zs = lax.rem(z + 8 - d, 8)
        to_sib(ga.at[core, zs], ga.at[core, zs], at_s.at[d], at_r.at[d]).wait_recv()
    start(to_sib(ga.at[core], ga.at[core], at_s.at[0], at_r.at[0]))
    pump(2, 1)
    pump(2, 2)
    pump(3, 0)
    attend(one, 1)
    to_sib(ga.at[1 - core], ga.at[1 - core], at_s.at[0], at_r.at[0]).wait_recv()
    ld[9].wait()
    for cc in range(2):
        for zz in range(8):
            at0 = (2 * zz + cc) * 32
            gaf[at0 : at0 + 32, :] = ga[cc, zz].astype(F32)
    a = jnp.concatenate([gaf[pl.ds(h, 32, stride=16), :] for h in range(GROUP)], axis=1).astype(BF16)
    terms = jnp.dot(a, w_v[...], preferred_element_type=F32)
    for t in range(N_TP):
        t_out[t, 0:4, :] = terms[4 * t : 4 * t + 4, 0 : DOUT // 2]
        t_out[t, 4:8, :] = terms[4 * t : 4 * t + 4, DOUT // 2 : DOUT]
    for d in range(1, N_TP):
        to = lax.rem(tp + d, N_TP)
        c = pltpu.make_async_remote_copy(
            src_ref=t_out.at[to], dst_ref=t_in.at[tp], send_sem=tp_s.at[d], recv_sem=tp_r.at[d],
            device_id={"tp": to}, device_id_type=MESH,
        )
        start(c)
    two = [pref(origin(0, 2)), pref(origin(1, 2))]
    attend(two, 0)
    pump(3, 1)
    pump(3, 2)
    pump(4, 0)

    ships = []
    ld[11].wait()
    for o, owner in enumerate((p, sib)):
        for j in range(4):
            src = lax.rem(owner + N_CTX - shift[role, j], N_CTX)
            mine = lax.rem(src, 2) == core
            f = gn[src // 2, TOK : TOK + FAC].astype(F32)
            for k in range(2):
                at0 = k * (TOK + FAC) + 16 * j
                raw = gn[src // 2, at0 : at0 + 16].astype(F32)
                code = raw * f[4 * k + j : 4 * k + j + 1, :]
                ship_out[o, k, 16 * j : 16 * j + 16] = jnp.where(mine, code, 0.0).astype(BF16)
        c = pltpu.make_async_remote_copy(
            src_ref=ship_out.at[o], dst_ref=ship_in.at[o], send_sem=sh_s.at[o], recv_sem=sh_r.at[o],
            device_id={"role": 1 - role, "ctx": owner}, device_id_type=MESH,
        )
        start(c)
        ships.append(c)
    eye = lax.broadcasted_iota(jnp.int32, (HD, HD), 0) == lax.broadcasted_iota(jnp.int32, (HD, HD), 1)
    backs = []

    def give(c, o, top):
        part_o[c] = (o[:, 0:HD] / o[:, HD:]).astype(BF16)
        lse = top + jnp.log2(o[:, HD:])
        for b in range(CHUNK // HD):
            x = jnp.where(eye, lse[b * HD : (b + 1) * HD], 0.0)
            part_s[c, b : b + 1, :] = jnp.sum(x, axis=0, keepdims=True)
        c1 = to_sib(part_o.at[c], back_o.at[c], po_s.at[c], po_r.at[c])
        c2 = to_sib(part_s.at[c], back_s.at[c], ps_s.at[c], ps_r.at[c])
        start(c1)
        start(c2)
        backs.append((c1, c2))

    def merge(c, o, top):
        mine = o[:, 0:HD] / o[:, HD:]
        lse = top + jnp.log2(o[:, HD:])
        other = []
        for b in range(CHUNK // HD):
            x = jnp.where(eye, jnp.broadcast_to(back_s[c, b : b + 1, :], (HD, HD)), 0.0)
            other.append(jnp.broadcast_to(jnp.sum(x, axis=1, keepdims=True), (HD, HD)))
        other = jnp.concatenate(other, axis=0)
        peak = jnp.maximum(lse, other)
        wa = jnp.exp2(lse - peak)
        wb = jnp.exp2(other - peak)
        res = ((mine * wa + back_o[c].astype(F32) * wb) / (wa + wb)).astype(BF16)
        for b in range(CHUNK // TOK):
            h = c * (CHUNK // TOK) + b
            out_attn[0, :, h * HD : (h + 1) * HD] = res[b * TOK : (b + 1) * TOK]

    attend(two, 1)
    three = [pref(origin(0, 3)), pref(origin(1, 3))]
    fresh = [(gn.at[i, 0:TOK], gn.at[i, TOK + FAC : NEWR]) for i in range(8)]
    attend(three, 1)
    attend(fresh, 1, masked=True, each=give)
    attend(three, 0)
    attend(fresh, 0, masked=True)

    total = t_out[tp]
    for d in range(1, N_TP):
        frm = lax.rem(tp + N_TP - d, N_TP)
        pltpu.make_async_remote_copy(
            src_ref=t_out.at[frm], dst_ref=t_in.at[frm], send_sem=tp_s.at[d], recv_sem=tp_r.at[d],
            device_id={"tp": frm}, device_id_type=MESH,
        ).wait_recv()
        total = total + t_in[frm]
    ld[10].wait()
    wide = jnp.concatenate([total[0:4], total[4:8]], axis=1)
    out_dec[0] = (res_v[...].astype(F32) + wide).astype(BF16)

    pump(4, 1)
    far = origin(0, 4)
    fars = []
    for i in (0, 1):
        c = to_sib(gp.at[far, :, i * HALF : (i + 1) * HALF], far_v.at[:, i * HALF : (i + 1) * HALF], far_s.at[i], far_r.at[i])
        start(c)
        fars.append(c)
    attend([pref(far)], 0)
    for c in fars:
        c.wait_recv()
    for x in backs:
        for c in x:
            c.wait_recv()
    attend([(far_v.at[0], far_v.at[1])], 0, each=merge)
    for c in ships:
        c.wait_recv()
    out_ship[0] = (ship_in[0].astype(F32) + ship_in[1].astype(F32)).astype(BF16)
    for c in sends:
        c.wait_send()


def hand_out(*refs):
    srcs, dsts, sem = refs[:3], refs[3:6], refs[6]
    cs = [pltpu.make_async_copy(a, b, sem.at[i]) for i, (a, b) in enumerate(zip(srcs, dsts))]
    for c in cs:
        c.start()
    for c in cs:
        c.wait()


def per_device(*args):
    args = list(args)
    args[3] = jnp.swapaxes(args[3], -1, -2)
    args[7] = jnp.swapaxes(args[7], -1, -2)
    out = main(*args)
    return pl.pallas_call(
        hand_out,
        out_shape=tuple(pltpu.HBM(x.shape, x.dtype) for x in out),
        in_specs=[pl.BlockSpec(memory_space=pltpu.VMEM)] * 3,
        out_specs=(pl.BlockSpec(memory_space=pltpu.HBM),) * 3,
        scratch_shapes=[pltpu.SemaphoreType.DMA((3,))],
    )(*[pltpu.with_memory_space_constraint(x, pltpu.VMEM) for x in out])


def main(*args):
    hb = pl.BlockSpec(memory_space=pltpu.HBM)
    dma = pltpu.SemaphoreType.DMA
    args = [pltpu.with_memory_space_constraint(a, pltpu.HBM) for a in args]
    return pl.pallas_call(
        kernel,
        out_shape=(
            pltpu.VMEM((1, TOK, GROUP * HD), BF16),
            pltpu.VMEM((1, 2, TOK, HD), BF16),
            pltpu.VMEM((1, 4, DOUT), BF16),
        ),
        in_specs=[hb] * len(args),
        out_specs=(pl.BlockSpec(memory_space=pltpu.VMEM),) * 3,
        scratch_shapes=[
            pltpu.VMEM((8, 2, PRE, HD), BF16),
            pltpu.VMEM((8, NEWR, HD), BF16),
            pltpu.VMEM((2, TOK, HD), BF16),
            pltpu.VMEM((2, 1, 4), jnp.int32),
            pltpu.VMEM((TOK, GROUP * HD), BF16),
            pltpu.VMEM((2 * ROWS, HD), BF16),
            pltpu.VMEM((2 * ROWS, HD), F32),
            pltpu.VMEM((2 * ROWS, 2 * HD), F32),
            pltpu.VMEM((2, GROUP * HD), BF16),
            pltpu.VMEM((32, HD), F32),
            pltpu.VMEM((2, 2, CACHE, HD), BF16),
            pltpu.VMEM((2, 2, 1, CACHE // CBLK), jnp.int32),
            pltpu.VMEM((2, 2, HD), BF16),
            pltpu.VMEM((2, 8, 32, HD), BF16),
            pltpu.VMEM((512, HD), F32),
            pltpu.VMEM((GROUP * HD, DOUT), BF16),
            pltpu.VMEM((N_TP, 8, DOUT // 2), F32),
            pltpu.VMEM((N_TP, 8, DOUT // 2), F32),
            pltpu.VMEM((4, DOUT), BF16),
            pltpu.VMEM((2, 2, TOK, HD), BF16),
            pltpu.VMEM((2, 2, TOK, HD), BF16),
            pltpu.VMEM((ROWS // CHUNK, CHUNK, HD), BF16),
            pltpu.VMEM((ROWS // CHUNK, 8, HD), F32),
            pltpu.VMEM((ROWS // CHUNK, CHUNK, HD), BF16),
            pltpu.VMEM((ROWS // CHUNK, 8, HD), F32),
            pltpu.VMEM((2, PRE, HD), BF16),
            pltpu.SMEM((2, 4), jnp.int32),
            pltpu.SMEM((1, 2), jnp.int32),
            dma((13,)),
            dma((22,)), dma((22,)),
            dma((1,)), dma((1,)),
            dma((8,)), dma((8,)),
            dma((8,)), dma((8,)),
            dma((2,)), dma((2,)),
            dma((3,)), dma((3,)),
            dma((3,)), dma((3,)),
            dma((2,)), dma((2,)),
        ],
        compiler_params=pltpu.CompilerParams(
            collective_id=0, has_side_effects=True, vmem_limit_bytes=48 * 2**20
        ),
    )(*args)


def solution(mesh):
    placed = (
        P("role", "ctx", "tp"),
        P("role", None, "ctx", "tp"),
        P("role", None, "ctx", "tp"),
        P("role", None, "ctx", "tp"),
        P(),
        P("role", "ctx", "tp"),
        P("role", None, "ctx", None, "tp"),
        P("role", None, "ctx", None, "tp"),
        P("role", "ctx"),
        P("role", None, "ctx", "tp"),
        P("tp", "ctx"),
        P("role", "tp", "ctx"),
    )
    return jax.shard_map(
        per_device,
        mesh=mesh,
        in_specs=placed,
        out_specs=(P("role", "ctx", "tp"), P("role", None, "ctx", "tp"), P("role", "tp", "ctx")),
        check_vma=False,
    )
```

time: 113 us -> 36 us (0.32)
  the two profiles are of different devices: /device:TPU:2 before, /device:TPU:1 now
where the time goes in v1:
time: 36 us; the launch traced here: 35.9 us
  Pallas kernels  35.3 us (98%)
  between operations  0.64 us (2%)
    pallas_call x1, Pallas kernels, main(): pl.pallas_call(kernel, out_shape=(pltpu.VMEM((1, TOK, GROUP * HD), BF16),...  34.6 us

profile of v1, /device:TPU:1, one launch (start us, length us, event | category | flops | bytes accessed | tf_op | source)
XLA Modules:
  0.0 35.9 jit_solution(6105605245709624249)
XLA Ops:
  0.6 34.6 %shard_map.139 = (bf16[1,64,1536]{2,1,0:T(8,128)(2,1)S(1)}, bf16[1,2,64,128]{3,2,1,0:T(8,128)(2,1)S(1)}, bf16[1,4,768]{2,1,0:T(4,128)(2,1)S(1)}) custom-call(bf16[1,64,1536]{2,1,0:T(8,128)(2,1)} %q_hbm.1, bf16[1,2,256,128]{3,2,1,0:T(8,128)(2,1)} %prefix.1, bf16[1,2,64,128]{3,2,1,0:T(8,128)(2,1)} %new.1, s32[1,2,1,4]{3,2,1,0:T(1,128)} %bitcast.7, ...), custom_call_target="tpu_custom_call" | custom-call | tf_op jit(solution)/shard_map/pallas_call | solution.py:389
  35.2 0.7 %shard_map.140 = (bf16[1,64,1536]{2,1,0:T(8,128)(2,1)}, bf16[1,2,64,128]{3,2,1,0:T(8,128)(2,1)}, bf16[1,4,768]{2,1,0:T(4,128)(2,1)}) custom-call(bf16[1,64,1536]{2,1,0:T(8,128)(2,1)S(1)} %get-tuple-element.6.refs_0_, bf16[1,2,64,128]{3,2,1,0:T(8,128)(2,1)S(1)} %get-tuple-element.7.refs_1_, bf16[1,4,768]{2,1,0:T(4,128)(2,1)S(1)} %get-tuple-element.8.refs_2_), custom_call_target="tpu_custom_call" | custom-call | tf_op jit(solution)/shard_map/pallas_call | solution.py:376

commit v2 on v1

--- a/solution.py
+++ b/solution.py
@@ -16,8 +16,6 @@
 ROWS = GROUP * TOK
 N_CTX = 16
 N_TP = 8
-FAC = 16
-NEWR = 2 * TOK + FAC
 CACHE = 2048
 CBLK = 128
 DOUT = 768
@@ -38,10 +36,10 @@
 def kernel(
     q_hbm, prefix, new, nexp, shift_in, dq, cache, cexp, clen_in, dnew, w, resid,
     out_attn, out_ship, out_dec,
-    gp, gn, nraw, ne, q_in, q_rows, m_ref, acc_ref,
-    dq_in, dq_rows, cache_v, ce, dn, ga, gaf, w_v, t_out, t_in, res_v, ship_out, ship_in,
+    gp, gn, ne, q_in, q_rows, m_ref, acc_ref,
+    dq_in, dq_rows, cache_v, ce, dn, ga, gb, gaf, w_v, t_out, t_in, res_v, ship_out, ship_in,
     part_o, part_s, back_o, back_s, far_v, shift, clen,
-    lsem, ring_s, ring_r, q_s, q_r, at_s, at_r, tp_s, tp_r, sh_s, sh_r, po_s, po_r, ps_s, ps_r, far_s, far_r,
+    lsem, ring_s, ring_r, q_s, q_r, at_s, at_r, tp_s, tp_r, sh_s, sh_r, po_s, po_r, ps_s, ps_r, far_s, far_r, near, nearer,
 ):
     role, p, tp = lax.axis_index("role"), lax.axis_index("ctx"), lax.axis_index("tp")
     core = lax.rem(p, 2)
@@ -49,17 +47,14 @@
     right, left = lax.rem(p + 2, N_CTX), lax.rem(p + N_CTX - 2, N_CTX)
     sib = p + 1 - 2 * core
 
+    y, x_lo = lax.rem(tp, 4), tp // 4
+    beside = [{"tp": x_lo * 4 + lax.rem(y + 1, 4)}, {"tp": x_lo * 4 + lax.rem(y + 3, 4)}, {"tp": (1 - x_lo) * 4 + y}]
     bar = pltpu.get_barrier_semaphore()
-    for d in range(1, 8):
-        pl.semaphore_signal(bar, inc=1, device_id={"ctx": lax.rem(p + 2 * d, N_CTX)}, device_id_type=MESH)
-    pl.semaphore_signal(bar, inc=1, device_id={"ctx": sib}, device_id_type=MESH)
-    for d in range(1, N_TP):
-        pl.semaphore_signal(bar, inc=1, device_id={"tp": lax.rem(tp + d, N_TP)}, device_id_type=MESH)
-    for c in (p, sib):
-        pl.semaphore_signal(bar, inc=1, device_id={"role": 1 - role, "ctx": c}, device_id_type=MESH)
+    for d in [{"ctx": right}, {"ctx": left}, {"ctx": sib}, {"role": 1 - role}] + beside:
+        pl.semaphore_signal(bar, inc=1, device_id=d, device_id_type=MESH)
 
     loads = [
-        (new.at[0], nraw), (nexp.at[0], ne), (prefix.at[0], gp.at[z]),
+        (new.at[0], gn.at[z]), (nexp.at[0], ne), (prefix.at[0], gp.at[z]),
         (dq.at[0], dq_in), (cexp.at[0], ce), (dnew.at[0], dn),
         (cache.at[0, 0], cache_v.at[0]), (cache.at[0, 1], cache_v.at[1]),
         (q_hbm.at[0], q_in), (w, w_v), (resid.at[0], res_v), (shift_in, shift), (clen_in, clen),
@@ -68,7 +63,7 @@
     for c in ld:
         c.start()
 
-    pl.semaphore_wait(bar, 17)
+    pl.semaphore_wait(bar, 7)
 
     dev = (right, left)
     kinds = {h: ((0, 1, 2), (0, 2, 1)) for h in (1, 2, 3)}
@@ -87,8 +82,8 @@
         if kd == 2:
             return gp.at[src, :, HALF:PRE]
         if kd == 3:
-            return gn.at[src, 0 : TOK + FAC]
-        return gn.at[src, TOK + FAC : NEWR]
+            return gn.at[src, 0]
+        return gn.at[src, 1]
 
     def origin(dr, h):
         return lax.rem(z + (8 - h if dr == 0 else h), 8)
@@ -109,7 +104,7 @@
     def post(j):
         for dr in (0, 1):
             kd = kinds[1][dr][j]
-            src = gn.at[z] if j == 0 else prefix.at[0, :, 0:HALF] if kd == 1 else prefix.at[0, :, HALF:PRE]
+            src = new.at[0] if j == 0 else prefix.at[0, :, 0:HALF] if kd == 1 else prefix.at[0, :, HALF:PRE]
             start(ring_copy(z, kd, dr, 1, src))
 
     def pump(h, j):
@@ -158,52 +153,60 @@
         total = jnp.sum(tot, axis=1, keepdims=True) + own
         o = jnp.dot(jnp.concatenate(pv, axis=1), cache_v[1, r], preferred_element_type=F32)
         o = o + own.astype(BF16).astype(F32) * vn
-        ga[core, z, 16 * r : 16 * r + 16] = (o / total).astype(BF16)
-
-    def attend(blocks, half, first=False, masked=False, each=None):
-        for c in range(ROWS // CHUNK):
-            rows = pl.ds(half * ROWS + c * CHUNK, CHUNK)
-            qc = q_rows[rows]
-            keys = jnp.concatenate([b[0][...] for b in blocks], axis=0)
-            vals = jnp.concatenate([b[1][...] for b in blocks], axis=0)
-            n = keys.shape[0]
-            s = lax.dot_general(qc, keys, NT, preferred_element_type=F32)
-            if masked:
-                col = lax.broadcasted_iota(jnp.int32, (CHUNK, n), 1)
-                key = (col // TOK) * (2 * TOK) + lax.rem(col, TOK) + core * TOK
-                tok = lax.rem(lax.broadcasted_iota(jnp.int32, (CHUNK, n), 0), TOK) + (sib if half else p) * TOK
-                s = jnp.where(key <= tok, s, NEG)
-            top = jnp.max(s, axis=1, keepdims=True) * SCALE2
+        fac = jnp.concatenate([jnp.zeros((12, 1), F32), jnp.exp2(-column(ne[r]))], axis=0)
+        row = lax.broadcasted_iota(jnp.int32, (16, HD), 0)
+        ga[z, 16 * r : 16 * r + 16] = jnp.where(row < GROUP, o / total, fac).astype(BF16)
+
+    def attend(blocks, half, first=False, fresh=False, each=None):
+        if fresh:
+            blocks = blocks + [(gn.at[i, 0], gn.at[i, 1]) for i in range(8)]
+        keys = jnp.concatenate([b[0][...] for b in blocks], axis=0)
+        n = keys.shape[0]
+        vals = jnp.concatenate([b[1][...] for b in blocks], axis=0)
+        vals = jnp.concatenate([vals, jnp.ones((n, HD), BF16)], axis=1)
+        chunks = [pl.ds(half * ROWS + c * CHUNK, CHUNK) for c in range(ROWS // CHUNK)]
+
+        def scores(c):
+            s = lax.dot_general(q_rows[chunks[c]], keys, NT, preferred_element_type=F32)
+            return [s[:, j : j + HD] for j in range(0, n, HD)]
+
+        s = scores(0)
+        for c, rows in enumerate(chunks):
+            later = scores(c + 1) if c + 1 < len(chunks) else None
+            if fresh:
+                lane = lax.broadcasted_iota(jnp.int32, (CHUNK, HD), 1)
+                key = (lane // TOK) * (2 * TOK) + lax.rem(lane, TOK) + core * TOK
+                tok = lax.rem(lax.broadcasted_iota(jnp.int32, (CHUNK, HD), 0), TOK) + (sib if half else p) * TOK
+                for j in range(4):
+                    i = len(s) - 4 + j
+                    s[i] = jnp.where(key + j * (4 * TOK) <= tok, s[i], NEG)
+            top = s[0]
+            for x in s[1:]:
+                top = jnp.maximum(top, x)
+            top = jnp.broadcast_to(jnp.max(top, axis=1, keepdims=True), (CHUNK, HD))
             if not first:
                 before = m_ref[rows]
-                top = jnp.maximum(before[:, 0:1], top)
-            e = jnp.exp2(s * SCALE2 - top).astype(BF16)
-            vals = jnp.concatenate([vals, jnp.ones((n, HD), BF16)], axis=1)
+                top = jnp.maximum(before, top)
+            e = jnp.concatenate([jnp.exp2((x - top) * SCALE2).astype(BF16) for x in s], axis=1)
             o = jnp.dot(e, vals, preferred_element_type=F32)
             if not first:
-                keep = jnp.exp2(before - top)
+                keep = jnp.exp2((before - top) * SCALE2)
                 o = o + acc_ref[rows] * jnp.concatenate([keep, keep], axis=1)
-            top = jnp.broadcast_to(top, (CHUNK, HD))
             if each is not None:
                 each(c, o, top)
             else:
                 acc_ref[rows] = o
                 m_ref[rows] = top
+            s = later
 
     def pref(src):
         return (gp.at[src, 0], gp.at[src, 1])
 
+    post(0)
     post(1)
     post(2)
-    ld[0].wait()
-    ld[1].wait()
-    gn[z, 0:TOK] = nraw[0]
-    gn[z, TOK + FAC : NEWR] = nraw[1]
-    fk = jnp.exp2(-column(ne[0]))
-    fv = jnp.exp2(-column(ne[1]))
-    fac = jnp.concatenate([fk, fv, jnp.zeros((8, 1), F32)], axis=0)
-    gn[z, TOK : TOK + FAC] = jnp.broadcast_to(fac, (FAC, HD)).astype(BF16)
-    post(0)
+    for d in beside + [{"ctx": sib}]:
+        pl.semaphore_signal(near, inc=1, device_id=d, device_id_type=MESH)
     part_s[...] = jnp.zeros(part_s.shape, F32)
     ld[8].wait()
     for h in range(GROUP):
@@ -216,41 +219,72 @@
     for r in range(2):
         for h in range(GROUP):
             dq_rows[16 * r + h : 16 * r + h + 1, :] = x[r : r + 1, h * HD : (h + 1) * HD]
-    for i in (4, 5, 6, 7, 12):
+    for i in (1, 4, 5, 6, 7, 12):
         ld[i].wait()
     decode(0)
     decode(1)
-    for d in range(1, 8):
-        c = pltpu.make_async_remote_copy(
-            src_ref=ga.at[core, z], dst_ref=ga.at[core, z], send_sem=at_s.at[d], recv_sem=at_r.at[d],
-            device_id={"ctx": lax.rem(p + 2 * d, N_CTX)}, device_id_type=MESH,
-        )
-        start(c)
+
+    def at_send(*steps):
+        for d in steps:
+            c = pltpu.make_async_remote_copy(
+                src_ref=ga.at[z], dst_ref=ga.at[z], send_sem=at_s.at[d], recv_sem=at_r.at[d],
+                device_id={"ctx": lax.rem(p + 2 * d, N_CTX)}, device_id_type=MESH,
+            )
+            start(c)
+
     pump(1, 0)
-    ld[2].wait()
-    attend([pref(z)], 0, first=True)
+    at_send(1, 7, 2, 6)
     pump(1, 1)
     pump(1, 2)
+    one = [pref(z), pref(origin(0, 1)), pref(origin(1, 1))]
+    ld[2].wait()
+    attend(one, 0, first=True)
+    pump(2, 0)
+    at_send(3, 5)
     q_copy.wait_recv()
-    attend([pref(z)], 1, first=True)
-    pump(2, 0)
-    one = [pref(origin(0, 1)), pref(origin(1, 1))]
-    attend(one, 0)
-
-    for d in range(1, 8):
-        zs = lax.rem(z + 8 - d, 8)
-        to_sib(ga.at[core, zs], ga.at[core, zs], at_s.at[d], at_r.at[d]).wait_recv()
-    start(to_sib(ga.at[core], ga.at[core], at_s.at[0], at_r.at[0]))
+    attend(one, 1, first=True)
     pump(2, 1)
     pump(2, 2)
     pump(3, 0)
-    attend(one, 1)
-    to_sib(ga.at[1 - core], ga.at[1 - core], at_s.at[0], at_r.at[0]).wait_recv()
+    at_send(4)
+    pl.semaphore_wait(near, 4)
+    for d in beside:
+        pl.semaphore_signal(nearer, inc=1, device_id=d, device_id_type=MESH)
+    two = [pref(origin(0, 2)), pref(origin(1, 2))]
+    attend(two, 0)
+    attend(two, 1)
+    pump(4, 0)
+    ld[0].wait()
+
+    for d in range(1, 8):
+        zs = lax.rem(z + 8 - d, 8)
+        to_sib(ga.at[zs], ga.at[zs], at_s.at[d], at_r.at[d]).wait_recv()
+    start(to_sib(ga, gb, at_s.at[0], at_r.at[0]))
+    ships = []
+    ld[11].wait()
+    for o, owner in enumerate((p, sib)):
+        for j in range(4):
+            src = lax.rem(owner + N_CTX - shift[role, j], N_CTX)
+            mine = lax.rem(src, 2) == core
+            for k in range(2):
+                f = ga[src // 2, 16 * k : 16 * k + 16].astype(F32)
+                raw = gn[src // 2, k, 16 * j : 16 * j + 16].astype(F32)
+                code = raw * f[GROUP + j : GROUP + j + 1, :]
+                ship_out[o, k, 16 * j : 16 * j + 16] = jnp.where(mine, code, 0.0).astype(BF16)
+        c = pltpu.make_async_remote_copy(
+            src_ref=ship_out.at[o], dst_ref=ship_in.at[o], send_sem=sh_s.at[o], recv_sem=sh_r.at[o],
+            device_id={"role": 1 - role, "ctx": owner}, device_id_type=MESH,
+        )
+        start(c)
+        ships.append(c)
+    pump(3, 1)
+    pump(3, 2)
+    pl.semaphore_wait(nearer, 3)
+    to_sib(ga, gb, at_s.at[0], at_r.at[0]).wait_recv()
     ld[9].wait()
-    for cc in range(2):
-        for zz in range(8):
-            at0 = (2 * zz + cc) * 32
-            gaf[at0 : at0 + 32, :] = ga[cc, zz].astype(F32)
+    for zz in range(8):
+        gaf[pl.ds(pl.multiple_of((2 * zz + core) * 32, 32), 32), :] = ga[zz].astype(F32)
+        gaf[pl.ds(pl.multiple_of((2 * zz + 1 - core) * 32, 32), 32), :] = gb[zz].astype(F32)
     a = jnp.concatenate([gaf[pl.ds(h, 32, stride=16), :] for h in range(GROUP)], axis=1).astype(BF16)
     terms = jnp.dot(a, w_v[...], preferred_element_type=F32)
     for t in range(N_TP):
@@ -263,36 +297,12 @@
             device_id={"tp": to}, device_id_type=MESH,
         )
         start(c)
-    two = [pref(origin(0, 2)), pref(origin(1, 2))]
-    attend(two, 0)
-    pump(3, 1)
-    pump(3, 2)
-    pump(4, 0)
-
-    ships = []
-    ld[11].wait()
-    for o, owner in enumerate((p, sib)):
-        for j in range(4):
-            src = lax.rem(owner + N_CTX - shift[role, j], N_CTX)
-            mine = lax.rem(src, 2) == core
-            f = gn[src // 2, TOK : TOK + FAC].astype(F32)
-            for k in range(2):
-                at0 = k * (TOK + FAC) + 16 * j
-                raw = gn[src // 2, at0 : at0 + 16].astype(F32)
-                code = raw * f[4 * k + j : 4 * k + j + 1, :]
-                ship_out[o, k, 16 * j : 16 * j + 16] = jnp.where(mine, code, 0.0).astype(BF16)
-        c = pltpu.make_async_remote_copy(
-            src_ref=ship_out.at[o], dst_ref=ship_in.at[o], send_sem=sh_s.at[o], recv_sem=sh_r.at[o],
-            device_id={"role": 1 - role, "ctx": owner}, device_id_type=MESH,
-        )
-        start(c)
-        ships.append(c)
     eye = lax.broadcasted_iota(jnp.int32, (HD, HD), 0) == lax.broadcasted_iota(jnp.int32, (HD, HD), 1)
     backs = []
 
     def give(c, o, top):
         part_o[c] = (o[:, 0:HD] / o[:, HD:]).astype(BF16)
-        lse = top + jnp.log2(o[:, HD:])
+        lse = top * SCALE2 + jnp.log2(o[:, HD:])
         for b in range(CHUNK // HD):
             x = jnp.where(eye, lse[b * HD : (b + 1) * HD], 0.0)
             part_s[c, b : b + 1, :] = jnp.sum(x, axis=0, keepdims=True)
@@ -304,7 +314,7 @@
 
     def merge(c, o, top):
         mine = o[:, 0:HD] / o[:, HD:]
-        lse = top + jnp.log2(o[:, HD:])
+        lse = top * SCALE2 + jnp.log2(o[:, HD:])
         other = []
         for b in range(CHUNK // HD):
             x = jnp.where(eye, jnp.broadcast_to(back_s[c, b : b + 1, :], (HD, HD)), 0.0)
@@ -318,14 +328,22 @@
             h = c * (CHUNK // TOK) + b
             out_attn[0, :, h * HD : (h + 1) * HD] = res[b * TOK : (b + 1) * TOK]
 
-    attend(two, 1)
     three = [pref(origin(0, 3)), pref(origin(1, 3))]
-    fresh = [(gn.at[i, 0:TOK], gn.at[i, TOK + FAC : NEWR]) for i in range(8)]
-    attend(three, 1)
-    attend(fresh, 1, masked=True, each=give)
-    attend(three, 0)
-    attend(fresh, 0, masked=True)
-
+    attend(three, 1, fresh=True, each=give)
+    attend(three, 0, fresh=True)
+    pump(4, 1)
+    far = origin(0, 4)
+    fars = []
+    for i in (0, 1):
+        c = to_sib(gp.at[far, :, i * HALF : (i + 1) * HALF], far_v.at[:, i * HALF : (i + 1) * HALF], far_s.at[i], far_r.at[i])
+        start(c)
+        fars.append(c)
+    for x in backs:
+        for c in x:
+            c.wait_recv()
+    for c in fars:
+        c.wait_recv()
+    attend([pref(far), (far_v.at[0], far_v.at[1])], 0, each=merge)
     total = t_out[tp]
     for d in range(1, N_TP):
         frm = lax.rem(tp + N_TP - d, N_TP)
@@ -338,20 +356,6 @@
     wide = jnp.concatenate([total[0:4], total[4:8]], axis=1)
     out_dec[0] = (res_v[...].astype(F32) + wide).astype(BF16)
 
-    pump(4, 1)
-    far = origin(0, 4)
-    fars = []
-    for i in (0, 1):
-        c = to_sib(gp.at[far, :, i * HALF : (i + 1) * HALF], far_v.at[:, i * HALF : (i + 1) * HALF], far_s.at[i], far_r.at[i])
-        start(c)
-        fars.append(c)
-    attend([pref(far)], 0)
-    for c in fars:
-        c.wait_recv()
-    for x in backs:
-        for c in x:
-            c.wait_recv()
-    attend([(far_v.at[0], far_v.at[1])], 0, each=merge)
     for c in ships:
         c.wait_recv()
     out_ship[0] = (ship_in[0].astype(F32) + ship_in[1].astype(F32)).astype(BF16)
@@ -397,8 +401,7 @@
         out_specs=(pl.BlockSpec(memory_space=pltpu.VMEM),) * 3,
         scratch_shapes=[
             pltpu.VMEM((8, 2, PRE, HD), BF16),
-            pltpu.VMEM((8, NEWR, HD), BF16),
-            pltpu.VMEM((2, TOK, HD), BF16),
+            pltpu.VMEM((8, 2, TOK, HD), BF16),
             pltpu.VMEM((2, 1, 4), jnp.int32),
             pltpu.VMEM((TOK, GROUP * HD), BF16),
             pltpu.VMEM((2 * ROWS, HD), BF16),
@@ -409,7 +412,8 @@
             pltpu.VMEM((2, 2, CACHE, HD), BF16),
             pltpu.VMEM((2, 2, 1, CACHE // CBLK), jnp.int32),
             pltpu.VMEM((2, 2, HD), BF16),
-            pltpu.VMEM((2, 8, 32, HD), BF16),
+            pltpu.VMEM((8, 32, HD), BF16),
+            pltpu.VMEM((8, 32, HD), BF16),
             pltpu.VMEM((512, HD), F32),
             pltpu.VMEM((GROUP * HD, DOUT), BF16),
             pltpu.VMEM((N_TP, 8, DOUT // 2), F32),
@@ -433,6 +437,8 @@
             dma((3,)), dma((3,)),
             dma((3,)), dma((3,)),
             dma((2,)), dma((2,)),
+            pltpu.SemaphoreType.REGULAR,
+            pltpu.SemaphoreType.REGULAR,
         ],
         compiler_params=pltpu.CompilerParams(
             collective_id=0, has_side_effects=True, vmem_limit_bytes=48 * 2**20

time: 36 us -> 34 us (0.944)
  Pallas kernels: 35.3 us -> 33.3 us
    pallas_call x1, Pallas kernels: 34.6 us -> 32.6 us  [main(): pl.pallas_call(kernel, out_shape=(pltpu.VMEM((1, TOK, GROUP * HD), BF16),...]
where the time goes in v2:
time: 34 us; the launch traced here: 33.9 us
  Pallas kernels  33.3 us (98%)
  between operations  0.64 us (2%)
    pallas_call x1, Pallas kernels, main(): pl.pallas_call(kernel, out_shape=(pltpu.VMEM((1, TOK, GROUP * HD), BF16),...  32.6 us
    pallas_call x1, Pallas kernels, per_device(): pl.pallas_call(hand_out, out_shape=tuple((pltpu.HBM(x.shape, x.dtype) for...  0.71 us

profile of v2, /device:TPU:1, one launch (start us, length us, event | category | flops | bytes accessed | tf_op | source)
XLA Modules:
  0.0 33.9 jit_solution(13774960707869064291)
XLA Ops:
  0.6 32.6 %shard_map.139 = (bf16[1,64,1536]{2,1,0:T(8,128)(2,1)S(1)}, bf16[1,2,64,128]{3,2,1,0:T(8,128)(2,1)S(1)}, bf16[1,4,768]{2,1,0:T(4,128)(2,1)S(1)}) custom-call(bf16[1,64,1536]{2,1,0:T(8,128)(2,1)} %q_hbm.1, bf16[1,2,256,128]{3,2,1,0:T(8,128)(2,1)} %prefix.1, bf16[1,2,64,128]{3,2,1,0:T(8,128)(2,1)} %new.1, s32[1,2,1,4]{3,2,1,0:T(1,128)} %bitcast.7, ...), custom_call_target="tpu_custom_call" | custom-call | tf_op jit(solution)/shard_map/pallas_call | solution.py:393
  33.2 0.7 %shard_map.140 = (bf16[1,64,1536]{2,1,0:T(8,128)(2,1)}, bf16[1,2,64,128]{3,2,1,0:T(8,128)(2,1)}, bf16[1,4,768]{2,1,0:T(4,128)(2,1)}) custom-call(bf16[1,64,1536]{2,1,0:T(8,128)(2,1)S(1)} %get-tuple-element.6.refs_0_, bf16[1,2,64,128]{3,2,1,0:T(8,128)(2,1)S(1)} %get-tuple-element.7.refs_1_, bf16[1,4,768]{2,1,0:T(4,128)(2,1)S(1)} %get-tuple-element.8.refs_2_), custom_call_target="tpu_custom_call" | custom-call | tf_op jit(solution)/shard_map/pallas_call | solution.py:380

commit v3 on v2

--- a/solution.py
+++ b/solution.py
@@ -39,7 +39,7 @@
     gp, gn, ne, q_in, q_rows, m_ref, acc_ref,
     dq_in, dq_rows, cache_v, ce, dn, ga, gb, gaf, w_v, t_out, t_in, res_v, ship_out, ship_in,
     part_o, part_s, back_o, back_s, far_v, shift, clen,
-    lsem, ring_s, ring_r, q_s, q_r, at_s, at_r, tp_s, tp_r, sh_s, sh_r, po_s, po_r, ps_s, ps_r, far_s, far_r, near, nearer,
+    lsem, ring_s, ring_r, q_s, q_r, at_s, at_r, tp_s, tp_r, sh_s, sh_r, po_s, po_r, ps_s, ps_r, far_s, far_r, near, z_sem,
 ):
     role, p, tp = lax.axis_index("role"), lax.axis_index("ctx"), lax.axis_index("tp")
     core = lax.rem(p, 2)
@@ -47,11 +47,26 @@
     right, left = lax.rem(p + 2, N_CTX), lax.rem(p + N_CTX - 2, N_CTX)
     sib = p + 1 - 2 * core
 
-    y, x_lo = lax.rem(tp, 4), tp // 4
-    beside = [{"tp": x_lo * 4 + lax.rem(y + 1, 4)}, {"tp": x_lo * 4 + lax.rem(y + 3, 4)}, {"tp": (1 - x_lo) * 4 + y}]
+    y, x = lax.rem(tp, 4), 2 * role + tp // 4
+    beside = [
+        (x < 3, {"role": (x + 1) // 2, "tp": lax.rem(x + 1, 2) * 4 + y}),
+        (x > 0, {"role": (x - 1) // 2, "tp": lax.rem(x + 3, 2) * 4 + y}),
+        (y < 3, {"tp": tp + 1}),
+        (y > 0, {"tp": tp - 1}),
+    ]
+    count = sum(there.astype(jnp.int32) for there, _ in beside)
+
+    def tell(sem):
+        for there, d in beside:
+
+            @pl.when(there)
+            def _(d=d):
+                pl.semaphore_signal(sem, inc=1, device_id=d, device_id_type=MESH)
+
     bar = pltpu.get_barrier_semaphore()
-    for d in [{"ctx": right}, {"ctx": left}, {"ctx": sib}, {"role": 1 - role}] + beside:
+    for d in ({"ctx": right}, {"ctx": left}, {"ctx": sib}):
         pl.semaphore_signal(bar, inc=1, device_id=d, device_id_type=MESH)
+    tell(bar)
 
     loads = [
         (new.at[0], gn.at[z]), (nexp.at[0], ne), (prefix.at[0], gp.at[z]),
@@ -60,10 +75,7 @@
         (q_hbm.at[0], q_in), (w, w_v), (resid.at[0], res_v), (shift_in, shift), (clen_in, clen),
     ]
     ld = [pltpu.make_async_copy(s, d, lsem.at[i]) for i, (s, d) in enumerate(loads)]
-    for c in ld:
-        c.start()
-
-    pl.semaphore_wait(bar, 7)
+    pl.semaphore_wait(bar, 3 + count)
 
     dev = (right, left)
     kinds = {h: ((0, 1, 2), (0, 2, 1)) for h in (1, 2, 3)}
@@ -96,6 +108,12 @@
         )
 
     sends = []
+    done = [0]
+
+    def drain(upto):
+        for c in sends[done[0] : upto]:
+            c.wait_send()
+        done[0] = max(done[0], upto)
 
     def start(c):
         c.start()
@@ -205,8 +223,12 @@
     post(0)
     post(1)
     post(2)
-    for d in beside + [{"ctx": sib}]:
-        pl.semaphore_signal(near, inc=1, device_id=d, device_id_type=MESH)
+    along = [{"ctx": right}, {"ctx": left}]
+    for d in along:
+        pl.semaphore_signal(z_sem.at[0], inc=1, device_id=d, device_id_type=MESH)
+    for i in (8, 3, 1, 4, 5, 12, 6, 7, 2, 0, 9, 10, 11):
+        ld[i].start()
+    tell(near.at[0])
     part_s[...] = jnp.zeros(part_s.shape, F32)
     ld[8].wait()
     for h in range(GROUP):
@@ -232,34 +254,42 @@
             )
             start(c)
 
+    def next_z(i, more):
+        pl.semaphore_wait(z_sem.at[i], 2)
+        if i < 2:
+            for d in along:
+                pl.semaphore_signal(z_sem.at[i + 1], inc=1, device_id=d, device_id_type=MESH)
+        at_send(*more)
+
+    next_z(0, (1, 7, 2, 6))
     pump(1, 0)
-    at_send(1, 7, 2, 6)
+    next_z(1, (3, 5))
+    pl.semaphore_wait(near.at[0], count)
+    tell(near.at[1])
     pump(1, 1)
     pump(1, 2)
+    next_z(2, (4,))
+    pl.semaphore_wait(near.at[1], count)
+    tell(near.at[2])
     one = [pref(z), pref(origin(0, 1)), pref(origin(1, 1))]
     ld[2].wait()
     attend(one, 0, first=True)
     pump(2, 0)
-    at_send(3, 5)
     q_copy.wait_recv()
     attend(one, 1, first=True)
+    old = len(sends)
     pump(2, 1)
     pump(2, 2)
     pump(3, 0)
-    at_send(4)
-    pl.semaphore_wait(near, 4)
-    for d in beside:
-        pl.semaphore_signal(nearer, inc=1, device_id=d, device_id_type=MESH)
     two = [pref(origin(0, 2)), pref(origin(1, 2))]
     attend(two, 0)
-    attend(two, 1)
-    pump(4, 0)
-    ld[0].wait()
-
     for d in range(1, 8):
         zs = lax.rem(z + 8 - d, 8)
         to_sib(ga.at[zs], ga.at[zs], at_s.at[d], at_r.at[d]).wait_recv()
     start(to_sib(ga, gb, at_s.at[0], at_r.at[0]))
+    attend(two, 1)
+    pump(4, 0)
+    ld[0].wait()
     ships = []
     ld[11].wait()
     for o, owner in enumerate((p, sib)):
@@ -277,9 +307,7 @@
         )
         start(c)
         ships.append(c)
-    pump(3, 1)
-    pump(3, 2)
-    pl.semaphore_wait(nearer, 3)
+    pl.semaphore_wait(near.at[2], count)
     to_sib(ga, gb, at_s.at[0], at_r.at[0]).wait_recv()
     ld[9].wait()
     for zz in range(8):
@@ -297,6 +325,10 @@
             device_id={"tp": to}, device_id_type=MESH,
         )
         start(c)
+    drain(old)
+    old = len(sends)
+    pump(3, 1)
+    pump(3, 2)
     eye = lax.broadcasted_iota(jnp.int32, (HD, HD), 0) == lax.broadcasted_iota(jnp.int32, (HD, HD), 1)
     backs = []
 
@@ -331,6 +363,8 @@
     three = [pref(origin(0, 3)), pref(origin(1, 3))]
     attend(three, 1, fresh=True, each=give)
     attend(three, 0, fresh=True)
+    drain(old)
+
     pump(4, 1)
     far = origin(0, 4)
     fars = []
@@ -359,8 +393,7 @@
     for c in ships:
         c.wait_recv()
     out_ship[0] = (ship_in[0].astype(F32) + ship_in[1].astype(F32)).astype(BF16)
-    for c in sends:
-        c.wait_send()
+    drain(len(sends))
 
 
 def hand_out(*refs):
@@ -437,8 +470,8 @@
             dma((3,)), dma((3,)),
             dma((3,)), dma((3,)),
             dma((2,)), dma((2,)),
-            pltpu.SemaphoreType.REGULAR,
-            pltpu.SemaphoreType.REGULAR,
+            pltpu.SemaphoreType.REGULAR((3,)),
+            pltpu.SemaphoreType.REGULAR((3,)),
         ],
         compiler_params=pltpu.CompilerParams(
             collective_id=0, has_side_effects=True, vmem_limit_bytes=48 * 2**20

time: 34 us -> 31.9 us (0.938)
  Pallas kernels: 33.3 us -> 31.2 us
    pallas_call x1, Pallas kernels: 32.6 us -> 30.5 us  [main(): pl.pallas_call(kernel, out_shape=(pltpu.VMEM((1, TOK, GROUP * HD), BF16),...]
where the time goes in v3:
time: 31.9 us
  Pallas kernels  31.2 us (98%)
  between operations  0.64 us (2%)
    pallas_call x1, Pallas kernels, main(): pl.pallas_call(kernel, out_shape=(pltpu.VMEM((1, TOK, GROUP * HD), BF16),...  30.5 us
    pallas_call x1, Pallas kernels, per_device(): pl.pallas_call(hand_out, out_shape=tuple((pltpu.HBM(x.shape, x.dtype) for...  0.71 us

profile of v3, /device:TPU:1, one launch (start us, length us, event | category | flops | bytes accessed | tf_op | source)
XLA Modules:
  0.0 31.9 jit_solution(6221410767385254929)
XLA Ops:
  0.6 30.5 %shard_map.139 = (bf16[1,64,1536]{2,1,0:T(8,128)(2,1)S(1)}, bf16[1,2,64,128]{3,2,1,0:T(8,128)(2,1)S(1)}, bf16[1,4,768]{2,1,0:T(4,128)(2,1)S(1)}) custom-call(bf16[1,64,1536]{2,1,0:T(8,128)(2,1)} %q_hbm.1, bf16[1,2,256,128]{3,2,1,0:T(8,128)(2,1)} %prefix.1, bf16[1,2,64,128]{3,2,1,0:T(8,128)(2,1)} %new.1, s32[1,2,1,4]{3,2,1,0:T(1,128)} %bitcast.7, ...), custom_call_target="tpu_custom_call" | custom-call | tf_op jit(solution)/shard_map/pallas_call | solution.py:426
  31.1 0.7 %shard_map.140 = (bf16[1,64,1536]{2,1,0:T(8,128)(2,1)}, bf16[1,2,64,128]{3,2,1,0:T(8,128)(2,1)}, bf16[1,4,768]{2,1,0:T(4,128)(2,1)}) custom-call(bf16[1,64,1536]{2,1,0:T(8,128)(2,1)S(1)} %get-tuple-element.6.refs_0_, bf16[1,2,64,128]{3,2,1,0:T(8,128)(2,1)S(1)} %get-tuple-element.7.refs_1_, bf16[1,4,768]{2,1,0:T(4,128)(2,1)S(1)} %get-tuple-element.8.refs_2_), custom_call_target="tpu_custom_call" | custom-call | tf_op jit(solution)/shard_map/pallas_call | solution.py:413

commit v4 on v3

--- a/solution.py
+++ b/solution.py
@@ -287,7 +287,11 @@
         zs = lax.rem(z + 8 - d, 8)
         to_sib(ga.at[zs], ga.at[zs], at_s.at[d], at_r.at[d]).wait_recv()
     start(to_sib(ga, gb, at_s.at[0], at_r.at[0]))
+    drain(old)
+    old = len(sends)
     attend(two, 1)
+    pump(3, 1)
+    pump(3, 2)
     pump(4, 0)
     ld[0].wait()
     ships = []
@@ -325,10 +329,6 @@
             device_id={"tp": to}, device_id_type=MESH,
         )
         start(c)
-    drain(old)
-    old = len(sends)
-    pump(3, 1)
-    pump(3, 2)
     eye = lax.broadcasted_iota(jnp.int32, (HD, HD), 0) == lax.broadcasted_iota(jnp.int32, (HD, HD), 1)
     backs = []
 

time: 31.9 us -> 30.8 us (0.966)
  Pallas kernels: 31.2 us -> 30.1 us
    pallas_call x1, Pallas kernels: 30.5 us -> 29.3 us  [main(): pl.pallas_call(kernel, out_shape=(pltpu.VMEM((1, TOK, GROUP * HD), BF16),...]
where the time goes in v4:
time: 30.8 us; the launch traced here: 30.7 us
  Pallas kernels  30.1 us (98%)
  between operations  0.64 us (2%)
    pallas_call x1, Pallas kernels, main(): pl.pallas_call(kernel, out_shape=(pltpu.VMEM((1, TOK, GROUP * HD), BF16),...  29.3 us
    pallas_call x1, Pallas kernels, per_device(): pl.pallas_call(hand_out, out_shape=tuple((pltpu.HBM(x.shape, x.dtype) for...  0.71 us

profile of v4, /device:TPU:1, one launch (start us, length us, event | category | flops | bytes accessed | tf_op | source)
XLA Modules:
  0.0 30.7 jit_solution(12532097981612211915)
XLA Ops:
  0.6 29.3 %shard_map.139 = (bf16[1,64,1536]{2,1,0:T(8,128)(2,1)S(1)}, bf16[1,2,64,128]{3,2,1,0:T(8,128)(2,1)S(1)}, bf16[1,4,768]{2,1,0:T(4,128)(2,1)S(1)}) custom-call(bf16[1,64,1536]{2,1,0:T(8,128)(2,1)} %q_hbm.1, bf16[1,2,256,128]{3,2,1,0:T(8,128)(2,1)} %prefix.1, bf16[1,2,64,128]{3,2,1,0:T(8,128)(2,1)} %new.1, s32[1,2,1,4]{3,2,1,0:T(1,128)} %bitcast.7, ...), custom_call_target="tpu_custom_call" | custom-call | tf_op jit(solution)/shard_map/pallas_call | solution.py:426
  30.0 0.7 %shard_map.140 = (bf16[1,64,1536]{2,1,0:T(8,128)(2,1)}, bf16[1,2,64,128]{3,2,1,0:T(8,128)(2,1)}, bf16[1,4,768]{2,1,0:T(4,128)(2,1)}) custom-call(bf16[1,64,1536]{2,1,0:T(8,128)(2,1)S(1)} %get-tuple-element.6.refs_0_, bf16[1,2,64,128]{3,2,1,0:T(8,128)(2,1)S(1)} %get-tuple-element.7.refs_1_, bf16[1,4,768]{2,1,0:T(4,128)(2,1)S(1)} %get-tuple-element.8.refs_2_), custom_call_target="tpu_custom_call" | custom-call | tf_op jit(solution)/shard_map/pallas_call | solution.py:413
